TPU v7x, 256 devices: a whole 4x4x8 slice. The times are simulated.
256 devices in a mesh: section: 8 (over z_lo, x), seq: 32 (over z_hi, y, core).
Axes of the slice: x: 4, y: 4, z: 8 (z_hi: 4, z_lo: 2; z = z_hi * 2 + z_lo), core: 2. Of those that a mesh axis runs over, the one named last changes fastest.
Arguments:
- queries: bfloat16 [8, 3072, 4096], P('section', 'seq'), may hold values from -120 to 120
- keys: bfloat16 [8, 3072, 4096], P('section', 'seq'), may hold values from -120 to 120
- values: bfloat16 [8, 3072, 4096], P('section', 'seq'), may hold values from -6 to 6
- norm_gains: float32 [2, 4096], replicated, may hold values from 1.2 to 2.5
Outputs:
- attended: bfloat16 [8, 3072, 4096], P('section', 'seq')
All inputs are finite; a program needn't handle non-finite values.
Results may differ from a plain program's by a relative error of at most 0.0014.
The roundings to bfloat16 on the way count: a program that leaves them out, or rounds other values in their place, can miss the bound.
Values may be sent and summed in bfloat16 or wider, within the bound.
No kernel may reach another device: no remote copies, remote signals or barrier semaphores. Data moves between devices by JAX's collectives and lax.ppermute only.
A program may use at most 128 MiB of HBM per device.

v0:
```python
import math

import jax
import jax.numpy as jnp
from jax import lax
from jax.experimental import pallas as pl
from jax.experimental.pallas import tpu as pltpu
from jax.sharding import PartitionSpec as P

HEAD_DIM = 128
RING = 4
CHIPS = RING * RING
EXPONENT_SCALE = math.log2(math.e) / math.sqrt(HEAD_DIM)
F32 = jnp.float32
BF16 = jnp.bfloat16
VMEM_LIMIT = 32 * 2**20
PREPARE_VMEM = 60 * 2**20
LAST_WITH_LAST = (((1,), (1,)), ((), ()))
VMEM = pl.BlockSpec(memory_space=pltpu.VMEM)
SMEM = pl.BlockSpec(memory_space=pltpu.SMEM)


def head_column(scalars, z, y, h):
    z = lax.rem(z + h * scalars[2], RING)
    return pl.multiple_of(((z * RING + y) * 2 + h) * HEAD_DIM, HEAD_DIM)


def norm_rows(rows, gain):
    wide = rows.astype(F32)
    power = jnp.mean(wide * wide, axis=-1, keepdims=True)
    return (wide * lax.rsqrt(power + 1e-06) * gain).astype(BF16)


def prepare_keys_values(scalars, keys, values, gain, rows_block=48):
    tokens, features = keys.shape

    def kernel(scalar_ref, key_ref, value_ref, gain_ref, out_ref, normed):
        normed[...] = norm_rows(key_ref[...], gain_ref[...])
        for c in range(CHIPS):
            for h in range(2):
                column = head_column(scalar_ref, c // RING, c % RING, h)
                out_ref[c, h, 0] = normed[:, pl.ds(column, HEAD_DIM)]
                out_ref[c, h, 1] = value_ref[:, pl.ds(column, HEAD_DIM)]

    rows_spec = pl.BlockSpec((rows_block, features), lambda i, s: (i, 0))
    return pl.pallas_call(
        kernel,
        grid_spec=pltpu.PrefetchScalarGridSpec(
            num_scalar_prefetch=1,
            grid=(tokens // rows_block,),
            in_specs=[rows_spec] * 2 + [pl.BlockSpec((1, features), lambda i, s: (0, 0))],
            out_specs=pl.BlockSpec(
                (CHIPS, 2, 2, rows_block, HEAD_DIM), lambda i, s: (0, 0, 0, i, 0)
            ),
            scratch_shapes=[pltpu.VMEM((rows_block, features), BF16)],
        ),
        out_shape=jax.ShapeDtypeStruct((CHIPS, 2, 2, tokens, HEAD_DIM), BF16),
        compiler_params=pltpu.CompilerParams(vmem_limit_bytes=PREPARE_VMEM),
        name="prepare_kv",
    )(scalars, keys, values, gain)


def prepare_queries(scalars, queries, gain):
    tokens, features = queries.shape

    def kernel(scalar_ref, query_ref, gain_ref, out_ref, normed):
        normed[...] = norm_rows(query_ref[...], gain_ref[...])
        for c in range(CHIPS):
            for h in range(2):
                column = head_column(scalar_ref, c // RING, c % RING, h)
                out_ref[c, h] = normed[:, pl.ds(column, HEAD_DIM)]

    return pl.pallas_call(
        kernel,
        in_specs=[SMEM] + [VMEM] * 2,
        out_specs=VMEM,
        out_shape=jax.ShapeDtypeStruct((CHIPS, 2, tokens, HEAD_DIM), BF16),
        scratch_shapes=[pltpu.VMEM((tokens, features), BF16)],
        compiler_params=pltpu.CompilerParams(vmem_limit_bytes=VMEM_LIMIT),
        name="prepare_q",
    )(scalars, queries, gain)


def collect(scalars, blocks):
    tokens = blocks.shape[2]

    def kernel(scalar_ref, block_ref, out_ref):
        for c in range(CHIPS):
            for h in range(2):
                column = head_column(scalar_ref, c // RING, c % RING, h)
                out_ref[:, pl.ds(column, HEAD_DIM)] = block_ref[c, h]

    return pl.pallas_call(
        kernel,
        in_specs=[SMEM, VMEM],
        out_specs=VMEM,
        out_shape=jax.ShapeDtypeStruct((tokens, CHIPS * 2 * HEAD_DIM), BF16),
        compiler_params=pltpu.CompilerParams(vmem_limit_bytes=VMEM_LIMIT),
        name="collect",
    )(scalars, blocks)


def attend(scalars, queries, pieces, rows_block=192, keys_block=512):
    tokens = queries.shape[2]
    keys_each = CHIPS * tokens
    per = keys_each // keys_block
    inner = rows_block // tokens
    blocks = CHIPS // inner
    rows_all = 2 * CHIPS * tokens
    cost = pl.CostEstimate(
        flops=4 * rows_all * 4 * keys_each * HEAD_DIM,
        bytes_accessed=2 * 2 * 2 * 4 * keys_each * HEAD_DIM,
        transcendentals=rows_all * 4 * keys_each,
    )

    def kernel(scalar_ref, query_ref, *refs):
        own, prior = refs[:2], refs[2:6]
        out_ref, scores_a, scores_b, top_a, top_b = refs[6:]

        def piece(h, c, which):
            b, t = divmod(c, per)
            rows = own[b][:, h, which] if b < 2 else prior[2 * b - 4 + h][:, which]
            return rows.reshape(keys_each, HEAD_DIM)[t * keys_block : (t + 1) * keys_block]

        def phase(ahead, behind, count):
            if ahead:
                scores_in, top_in, h_in, r_in = ahead
                query = jnp.concatenate(
                    [query_ref[r_in * inner + j, h_in] for j in range(inner)], axis=0
                )
                top = None
            if behind:
                scores_out, top_out, h_out, r_out = behind
                shift = jnp.max(top_out[...], axis=1, keepdims=True) * EXPONENT_SCALE
                shift = jnp.broadcast_to(shift, (rows_block, HEAD_DIM))
                total = None
                mixed = None
            for c in range(count):
                base = c * keys_block
                if ahead:
                    raw = lax.dot_general(
                        query, piece(h_in, c, 0), LAST_WITH_LAST, preferred_element_type=F32
                    )
                    scores_in[:, base : base + keys_block] = raw
                    for j in range(0, keys_block, 128):
                        part = raw[:, j : j + 128]
                        top = part if top is None else jnp.maximum(top, part)
                if behind:
                    weights = []
                    for j in range(base, base + keys_block, 128):
                        expo = jnp.exp2(scores_out[:, j : j + 128] * EXPONENT_SCALE - shift)
                        total = expo if total is None else total + expo
                        weights.append(expo.astype(BF16))
                    part = jnp.dot(
                        jnp.concatenate(weights, axis=1),
                        piece(h_out, c, 1),
                        preferred_element_type=F32,
                    )
                    mixed = part if mixed is None else mixed + part
            if ahead:
                top_in[...] = top
            if behind:
                total = jnp.sum(total, axis=1, keepdims=True)
                result = (mixed / total).astype(BF16)
                for j in range(inner):
                    out_ref[r_out * inner + j, h_out] = result[j * tokens : (j + 1) * tokens]

        def whole(count):
            a, b = (scores_a, top_a), (scores_b, top_b)
            phase(a + (0, 0), None, count)

            def step(r, carry):
                phase(b + (1, r), a + (0, r), count)
                phase(a + (0, r + 1), b + (1, r), count)
                return carry

            lax.fori_loop(0, blocks - 1, step, 0)
            phase(b + (1, blocks - 1), a + (0, blocks - 1), count)
            phase(None, b + (1, blocks - 1), count)

        @pl.when(scalar_ref[3] > 0)
        def _():
            whole(4 * per)

        @pl.when(scalar_ref[3] == 0)
        def _():
            whole(2 * per)

    return pl.pallas_call(
        kernel,
        in_specs=[SMEM] + [VMEM] * 7,
        out_specs=VMEM,
        out_shape=jax.ShapeDtypeStruct(queries.shape, BF16),
        scratch_shapes=[
            pltpu.VMEM((rows_block, 4 * keys_each), F32),
            pltpu.VMEM((rows_block, 4 * keys_each), F32),
            pltpu.VMEM((rows_block, HEAD_DIM), F32),
            pltpu.VMEM((rows_block, HEAD_DIM), F32),
        ],
        cost_estimate=cost,
        compiler_params=pltpu.CompilerParams(vmem_limit_bytes=VMEM_LIMIT),
        name="attend",
    )(scalars, queries, *pieces)


def local(queries, keys, values, norm_gains):
    seq = lax.axis_size("seq")
    sections = lax.axis_size("section")
    here = lax.axis_index("seq")
    section = lax.axis_index("section")
    late = (section >= sections // 2).astype(jnp.int32)
    has_prior = (section > 0).astype(jnp.int32)
    scalars = jnp.stack([here // 8, here % 8 // 2, late, has_prior]).astype(jnp.int32)
    same_core = [[2 * p + c for p in range(CHIPS)] for c in range(2)]
    fence = lax.optimization_barrier

    def exchange(x):
        return lax.all_to_all(
            x, "seq", split_axis=0, concat_axis=0, tiled=True, axis_index_groups=same_core
        )

    def swap(x):
        return lax.ppermute(x, "seq", [(i, i ^ 1) for i in range(seq)])

    def passed_on(x, h):
        route = []
        for s in range(sections - 1):
            back = 8 * h if s + 1 == sections // 2 else 0
            for i in range(seq):
                route.append((s * seq + i, (s + 1) * seq + (i - back) % seq))
        return lax.ppermute(x, ("section", "seq"), route)

    own = exchange(prepare_keys_values(scalars, keys[0], values[0], norm_gains[1:2]))
    query_sent = prepare_queries(scalars, queries[0], norm_gains[0:1])
    query_sent, own = fence((query_sent, own))
    prior = [passed_on(own[:, h], h) for h in range(2)]
    head_queries = exchange(query_sent)
    own_other = swap(own)
    pieces = (own, own_other, *prior, *[swap(x) for x in prior])
    back = exchange(attend(scalars, head_queries, pieces))
    return collect(scalars, back)[None]


def solution(mesh):
    return jax.shard_map(
        local,
        mesh=mesh,
        in_specs=(
            P("section", "seq", None),
            P("section", "seq", None),
            P("section", "seq", None),
            P(),
        ),
        out_specs=P("section", "seq", None),
        check_vma=False,
    )
```

profile of v0, /device:TPU:6, one launch (start us, length us, event | category | flops | bytes accessed | tf_op | source)
XLA Modules:
  0.0 167.4 jit_solution(762664139941035184)
XLA Ops:
  0.0 1.5 fusion
  1.5 0.6 pad_add_fusion.scalar_ref
  2.1 3.4 %prepare_kv.1 = bf16[16,2,2,96,128]{4,3,2,1,0:T(8,128)(2,1)} custom-call(s32[4]{0:T(128)} %pad_add_fusion.scalar_ref, bf16[96,4096]{1,0:T(8,128)(2,1)} %bitcast.13, bf16[96,4096]{1,0:T(8,128)(2,1)} %bitcast.14, f32[1,4096]{1,0:T(1,128)} %get-tuple-element.11.gain_ref), custom_call_target="tpu_custom_call" | custom-call | tf_op jit(solution)/shard_map/prepare_kv/pallas_call | solution.py:46
  5.5 0.0 copy-start
  5.5 0.0 copy-start.1
  5.5 11.3 %all-to-all-start = ((bf16[16,2,2,96,128]{4,3,2,1,0:T(8,128)(2,1)}), bf16[16,2,2,96,128]{4,3,2,1,0:T(8,128)(2,1)S(1)}, u32[]{:S(2)}, u32[]{:S(2)}) async-start(bf16[16,2,2,96,128]{4,3,2,1,0:T(8,128)(2,1)} %prepare_kv.1), calls=%async_computation | async-start | bytes 3145728 | tf_op jit(solution)/shard_map/all_to_all | solution.py:218
  16.8 0.0 copy-done
  16.8 0.0 copy-done.1
  16.9 2.1 %prepare_q.1 = bf16[16,2,96,128]{3,2,1,0:T(8,128)(2,1)} custom-call(s32[4]{0:T(128)S(1)} %copy-done.1, bf16[96,4096]{1,0:T(8,128)(2,1)S(1)} %bitcast.12, f32[1,4096]{1,0:T(1,128)S(1)} %get-tuple-element.12.gain_ref), custom_call_target="tpu_custom_call" | custom-call | tf_op jit(solution)/shard_map/prepare_q/pallas_call | solution.py:73
  18.9 37.1 %all-to-all-done.refs_0_ = bf16[16,2,2,96,128]{4,3,2,1,0:T(8,128)(2,1)S(1)} async-done(((bf16[16,2,2,96,128]{4,3,2,1,0:T(8,128)(2,1)}), bf16[16,2,2,96,128]{4,3,2,1,0:T(8,128)(2,1)S(1)}, u32[]{:S(2)}, u32[]{:S(2)}) %all-to-all-start) | async-done | bytes 1572896 | tf_op jit(solution)/shard_map/all_to_all | solution.py:218
  56.1 1.2 slice_bitcast_fusion
  57.3 5.0 %collective-permute-start.2 = (bf16[16,2,96,128]{3,2,1,0:T(8,128)(2,1)}, bf16[16,2,96,128]{3,2,1,0:T(8,128)(2,1)S(1)}, u32[]{:S(2)}, u32[]{:S(2)}) collective-permute-start(bf16[16,2,96,128]{3,2,1,0:T(8,128)(2,1)} %get-tuple-element.9), channel_id=1, source_target_pairs={{0,32},{1,33},{2,34},{3,35},{4,36},{5,37},{6,38},{7,39},{8,40},{9,... | collective-permute-start | bytes 2359304 | tf_op jit(solution)/shard_map/ppermute | solution.py:231
  62.3 2.5 %collective-permute-start.1 = (bf16[16,2,96,128]{3,2,1,0:T(8,128)(2,1)}, bf16[16,2,96,128]{3,2,1,0:T(8,128)(2,1)}, u32[]{:S(2)}, u32[]{:S(2)}) collective-permute-start(bf16[16,2,96,128]{3,2,1,0:T(8,128)(2,1)} %get-tuple-element.10), channel_id=1, source_target_pairs={{0,32},{1,33},{2,34},{3,35},{4,36},{5,37},{6,38},{7,39},{8,40},{9,... | collective-permute-start | bytes 2359304 | tf_op jit(solution)/shard_map/ppermute | solution.py:231
  64.8 0.1 collective-permute-start
  64.9 4.5 %all-to-all-start.1 = ((bf16[16,2,96,128]{3,2,1,0:T(8,128)(2,1)}), bf16[16,2,96,128]{3,2,1,0:T(8,128)(2,1)S(1)}, u32[]{:S(2)}, u32[]{:S(2)}) async-start(bf16[16,2,96,128]{3,2,1,0:T(8,128)(2,1)} %prepare_q.1), calls=%async_computation.1 | async-start | bytes 1572864 | tf_op jit(solution)/shard_map/all_to_all | solution.py:218
  69.4 29.8 %collective-permute-done.2.refs_3_ = bf16[16,2,96,128]{3,2,1,0:T(8,128)(2,1)S(1)} collective-permute-done((bf16[16,2,96,128]{3,2,1,0:T(8,128)(2,1)}, bf16[16,2,96,128]{3,2,1,0:T(8,128)(2,1)S(1)}, u32[]{:S(2)}, u32[]{:S(2)}) %collective-permute-start.2) | collective-permute-done | bytes 786464 | tf_op jit(solution)/shard_map/ppermute | solution.py:231
  99.2 0.0 collective-permute-start.4
  99.2 0.0 collective-permute-done.1.refs_2_
  99.2 0.5 collective-permute-start.3
  99.8 8.8 %all-to-all-done.1.query_ref = bf16[16,2,96,128]{3,2,1,0:T(8,128)(2,1)S(1)} async-done(((bf16[16,2,96,128]{3,2,1,0:T(8,128)(2,1)}), bf16[16,2,96,128]{3,2,1,0:T(8,128)(2,1)S(1)}, u32[]{:S(2)}, u32[]{:S(2)}) %all-to-all-start.1) | async-done | bytes 786464 | tf_op jit(solution)/shard_map/all_to_all | solution.py:218
  108.5 0.0 collective-permute-done.4.refs_5_
  108.5 0.0 collective-permute-done.3.refs_4_
  108.5 0.0 collective-permute-done.refs_1_
  108.5 31.7 %attend.1 = bf16[16,2,96,128]{3,2,1,0:T(8,128)(2,1)S(1)} custom-call(s32[4]{0:T(128)S(1)} %copy-done.1, bf16[16,2,96,128]{3,2,1,0:T(8,128)(2,1)S(1)} %all-to-all-done.1.query_ref, bf16[16,2,2,96,128]{4,3,2,1,0:T(8,128)(2,1)S(1)} %all-to-all-done.refs_0_, bf16[16,2,2,96,128]{4,3,2,1,0:T(8,128)(2,1)} %collective-permute-done.refs_1_, ...), custom_call_target="tpu_custom_call" | custom-call | flops 9663676416 | bytes 6291456 | tf_op jit(solution)/shard_map/attend/pallas_call | solution.py:189
  140.3 25.5 %all_to_all.15.block_ref = bf16[16,2,96,128]{3,2,1,0:T(8,128)(2,1)S(1)} all-to-all(bf16[16,2,96,128]{3,2,1,0:T(8,128)(2,1)S(1)} %attend.1), channel_id=1, replica_groups={{0,2,4,6,8,10,12,14,16,18,20,22,24,26,28,30},{1,3,5,7,9,11,13,15,17,19,..., dimensions={0} | all-to-all | bytes 1572864 | tf_op jit(solution)/shard_map/all_to_all | solution.py:218
  165.8 1.6 collect.1
Async XLA Ops:
  5.5 11.3 %copy-start = (bf16[1,96,4096]{2,1,0:T(8,128)(2,1)S(1)}, bf16[1,96,4096]{2,1,0:T(8,128)(2,1)}, u32[]{:S(2)}) copy-start(bf16[1,96,4096]{2,1,0:T(8,128)(2,1)} %param.4) | copy-start | bytes 2359300
  5.5 11.4 %copy-start.1 = (s32[4]{0:T(128)S(1)}, s32[4]{0:T(128)}, u32[]{:S(2)}) copy-start(s32[4]{0:T(128)} %pad_add_fusion.scalar_ref) | copy-start | bytes 52
  5.5 50.6 %all-to-all-start = ((bf16[16,2,2,96,128]{4,3,2,1,0:T(8,128)(2,1)}), bf16[16,2,2,96,128]{4,3,2,1,0:T(8,128)(2,1)S(1)}, u32[]{:S(2)}, u32[]{:S(2)}) async-start(bf16[16,2,2,96,128]{4,3,2,1,0:T(8,128)(2,1)} %prepare_kv.1), calls=%async_computation | async-start | bytes 3145728 | tf_op jit(solution)/shard_map/all_to_all | solution.py:218
  57.3 41.9 %collective-permute-start.2 = (bf16[16,2,96,128]{3,2,1,0:T(8,128)(2,1)}, bf16[16,2,96,128]{3,2,1,0:T(8,128)(2,1)S(1)}, u32[]{:S(2)}, u32[]{:S(2)}) collective-permute-start(bf16[16,2,96,128]{3,2,1,0:T(8,128)(2,1)} %get-tuple-element.9), channel_id=1, source_target_pairs={{0,32},{1,33},{2,34},{3,35},{4,36},{5,37},{6,38},{7,39},{8,40},{9,... | collective-permute-start | bytes 2359304 | tf_op jit(solution)/shard_map/ppermute | solution.py:231
  62.3 37.0 %collective-permute-start.1 = (bf16[16,2,96,128]{3,2,1,0:T(8,128)(2,1)}, bf16[16,2,96,128]{3,2,1,0:T(8,128)(2,1)}, u32[]{:S(2)}, u32[]{:S(2)}) collective-permute-start(bf16[16,2,96,128]{3,2,1,0:T(8,128)(2,1)} %get-tuple-element.10), channel_id=1, source_target_pairs={{0,32},{1,33},{2,34},{3,35},{4,36},{5,37},{6,38},{7,39},{8,40},{9,... | collective-permute-start | bytes 2359304 | tf_op jit(solution)/shard_map/ppermute | solution.py:231
  64.8 43.7 %collective-permute-start = (bf16[16,2,2,96,128]{4,3,2,1,0:T(8,128)(2,1)S(1)}, bf16[16,2,2,96,128]{4,3,2,1,0:T(8,128)(2,1)}, u32[]{:S(2)}, u32[]{:S(2)}) collective-permute-start(bf16[16,2,2,96,128]{4,3,2,1,0:T(8,128)(2,1)S(1)} %all-to-all-done.refs_0_), channel_id=1, source_target_pairs={{0,1},{1,0},{2,3},{3,2},{4,5},{5,4},{6,7},{7,6},{8,9},{9,8},{10,11... | collective-permute-start | bytes 4718600 | tf_op jit(solution)/shard_map/ppermute | solution.py:223
  64.9 43.6 %all-to-all-start.1 = ((bf16[16,2,96,128]{3,2,1,0:T(8,128)(2,1)}), bf16[16,2,96,128]{3,2,1,0:T(8,128)(2,1)S(1)}, u32[]{:S(2)}, u32[]{:S(2)}) async-start(bf16[16,2,96,128]{3,2,1,0:T(8,128)(2,1)} %prepare_q.1), calls=%async_computation.1 | async-start | bytes 1572864 | tf_op jit(solution)/shard_map/all_to_all | solution.py:218
  99.2 9.3 %collective-permute-start.4 = (bf16[16,2,96,128]{3,2,1,0:T(8,128)(2,1)S(1)}, bf16[16,2,96,128]{3,2,1,0:T(8,128)(2,1)}, u32[]{:S(2)}, u32[]{:S(2)}) collective-permute-start(bf16[16,2,96,128]{3,2,1,0:T(8,128)(2,1)S(1)} %collective-permute-done.2.refs_3_), channel_id=1, source_target_pairs={{0,1},{1,0},{2,3},{3,2},{4,5},{5,4},{6,7},{7,6},{8,9},{9,8},{10,11... | collective-permute-start | bytes 2359304 | tf_op jit(solution)/shard_map/ppermute | solution.py:223
  99.2 9.3 %collective-permute-start.3 = (bf16[16,2,96,128]{3,2,1,0:T(8,128)(2,1)}, bf16[16,2,96,128]{3,2,1,0:T(8,128)(2,1)}, u32[]{:S(2)}, u32[]{:S(2)}) collective-permute-start(bf16[16,2,96,128]{3,2,1,0:T(8,128)(2,1)} %collective-permute-done.1.refs_2_), channel_id=1, source_target_pairs={{0,1},{1,0},{2,3},{3,2},{4,5},{5,4},{6,7},{7,6},{8,9},{9,8},{10,11... | collective-permute-start | bytes 2359304 | tf_op jit(solution)/shard_map/ppermute | solution.py:223
where the time goes:
time: 168 us; the launch traced here: 167 us
  waiting for transfers between devices  75.7 us (45%)
  Pallas kernels  38.8 us (23%)
  blocking collectives  25.5 us (15%)
  starting transfers between devices  24 us (14%)
  local copies, waits for them, and re-layouts  2.71 us (2%)
    all_to_all x2, waiting for transfers between devices, exchange(): lax.all_to_all(x, 'seq', split_axis=0, concat_axis=0, tiled=True, axis_in...  45.9 us
    pallas_call x1, Pallas kernels, attend(): pl.pallas_call(kernel, in_specs=[SMEM] + [VMEM] * 7, out_specs=VMEM, out_...  31.7 us
    ppermute x2, waiting for transfers between devices, passed_on(): return lax.ppermute(x, ('section', 'seq'), route)  29.8 us
    all_to_all x1, blocking collectives, exchange(): lax.all_to_all(x, 'seq', split_axis=0, concat_axis=0, tiled=True, axis_in...  25.5 us
    all_to_all x2, starting transfers between devices, exchange(): lax.all_to_all(x, 'seq', split_axis=0, concat_axis=0, tiled=True, axis_in...  15.9 us
    ppermute x2, starting transfers between devices, passed_on(): return lax.ppermute(x, ('section', 'seq'), route)  7.47 us
    pallas_call x1, Pallas kernels, prepare_keys_values(): pl.pallas_call(kernel, grid_spec=pltpu.PrefetchScalarGridSpec(num_scalar_...  3.4 us
  transfers between devices with their start and end apart: 7, of which 3 were waited for; matrix products, arithmetic and copies ran while one was open for 0% of the time, Pallas kernels for 1%

commit v1 on v0

v1 whole, which is shorter than its diff:
```python
import math

import jax
import jax.numpy as jnp
from jax import lax
from jax.experimental import pallas as pl
from jax.experimental.pallas import tpu as pltpu
from jax.sharding import PartitionSpec as P

HEAD_DIM = 128
RING = 4
CHIPS = RING * RING
EXPONENT_SCALE = math.log2(math.e) / math.sqrt(HEAD_DIM)
F32 = jnp.float32
BF16 = jnp.bfloat16
VMEM_LIMIT = 28 * 2**20
PREPARE_VMEM = 60 * 2**20
LAST_WITH_LAST = (((1,), (1,)), ((), ()))
VMEM = pl.BlockSpec(memory_space=pltpu.VMEM)
SMEM = pl.BlockSpec(memory_space=pltpu.SMEM)


def head_column(scalars, z, y, h):
    z = lax.rem(z + h * scalars[2], RING)
    return pl.multiple_of(((z * RING + y) * 2 + h) * HEAD_DIM, HEAD_DIM)


def norm_rows(rows, gain):
    wide = rows.astype(F32)
    power = jnp.mean(wide * wide, axis=-1, keepdims=True)
    return (wide * lax.rsqrt(power + 1e-06) * gain).astype(BF16)


def prepare(scalars, queries, keys, values, gains, rows_block=48):
    tokens, features = keys.shape

    def kernel(scalar_ref, query_ref, key_ref, value_ref, gain_ref, first_ref, second_ref, key_norm, query_norm):
        key_norm[...] = norm_rows(key_ref[...], gain_ref[1:2, :])
        query_norm[...] = norm_rows(query_ref[...], gain_ref[0:1, :])
        for c in range(CHIPS):
            for h in range(2):
                at = pl.ds(head_column(scalar_ref, c // RING, c % RING, h), HEAD_DIM)
                kv_ref = second_ref if h else first_ref
                kv_ref[c, 0] = key_norm[:, at]
                kv_ref[c, 1] = value_ref[:, at]
                first_ref[c, 2 + h] = query_norm[:, at]

    rows_spec = pl.BlockSpec((rows_block, features), lambda i, s: (i, 0))

    def out_spec(n):
        return pl.BlockSpec((CHIPS, n, rows_block, HEAD_DIM), lambda i, s: (0, 0, i, 0))

    return pl.pallas_call(
        kernel,
        grid_spec=pltpu.PrefetchScalarGridSpec(
            num_scalar_prefetch=1,
            grid=(tokens // rows_block,),
            in_specs=[rows_spec] * 3 + [pl.BlockSpec((2, features), lambda i, s: (0, 0))],
            out_specs=[out_spec(4), out_spec(2)],
            scratch_shapes=[pltpu.VMEM((rows_block, features), BF16)] * 2,
        ),
        out_shape=[
            jax.ShapeDtypeStruct((CHIPS, n, tokens, HEAD_DIM), BF16) for n in (4, 2)
        ],
        compiler_params=pltpu.CompilerParams(vmem_limit_bytes=PREPARE_VMEM),
        name="prepare",
    )(scalars, queries, keys, values, gains)


def collect(scalars, blocks):
    tokens = blocks.shape[2]

    def kernel(scalar_ref, block_ref, out_ref):
        for c in range(CHIPS):
            for h in range(2):
                column = head_column(scalar_ref, c // RING, c % RING, h)
                out_ref[:, pl.ds(column, HEAD_DIM)] = block_ref[c, h]

    return pl.pallas_call(
        kernel,
        in_specs=[SMEM, VMEM],
        out_specs=VMEM,
        out_shape=jax.ShapeDtypeStruct((tokens, CHIPS * 2 * HEAD_DIM), BF16),
        compiler_params=pltpu.CompilerParams(vmem_limit_bytes=VMEM_LIMIT),
        name="collect",
    )(scalars, blocks)


def attend(scalars, queries, h, pieces, beside=None, rows_block=192, keys_block=512):
    tokens = queries.shape[2]
    keys_each = CHIPS * tokens
    per = keys_each // keys_block
    inner = rows_block // tokens
    blocks = CHIPS // inner
    rows_all = CHIPS * tokens
    cost = pl.CostEstimate(
        flops=4 * rows_all * 4 * keys_each * HEAD_DIM,
        bytes_accessed=2 * 2 * 4 * keys_each * HEAD_DIM,
        transcendentals=rows_all * 4 * keys_each,
    )

    def kernel(scalar_ref, query_ref, *refs):
        kv = refs[:4]
        out_ref, scores_a, scores_b, top_a, top_b = refs[-5:]

        def piece(c, which):
            b, t = divmod(c, per)
            rows = kv[b][:, which].reshape(keys_each, HEAD_DIM)
            return rows[t * keys_block : (t + 1) * keys_block]

        def phase(ahead, behind, count):
            if ahead:
                scores_in, top_in, r_in = ahead
                query = jnp.concatenate(
                    [query_ref[r_in * inner + j, 2 + h] for j in range(inner)], axis=0
                )
                top = None
            if behind:
                scores_out, top_out, r_out = behind
                shift = jnp.max(top_out[...], axis=1, keepdims=True) * EXPONENT_SCALE
                shift = jnp.broadcast_to(shift, (rows_block, HEAD_DIM))
                total = None
                mixed = None
            for c in range(count):
                base = c * keys_block
                if ahead:
                    raw = lax.dot_general(
                        query, piece(c, 0), LAST_WITH_LAST, preferred_element_type=F32
                    )
                    scores_in[:, base : base + keys_block] = raw
                    for j in range(0, keys_block, 128):
                        part = raw[:, j : j + 128]
                        top = part if top is None else jnp.maximum(top, part)
                if behind:
                    weights = []
                    for j in range(base, base + keys_block, 128):
                        expo = jnp.exp2(scores_out[:, j : j + 128] * EXPONENT_SCALE - shift)
                        total = expo if total is None else total + expo
                        weights.append(expo.astype(BF16))
                    part = jnp.dot(
                        jnp.concatenate(weights, axis=1),
                        piece(c, 1),
                        preferred_element_type=F32,
                    )
                    mixed = part if mixed is None else mixed + part
            if ahead:
                top_in[...] = top
            if behind:
                total = jnp.sum(total, axis=1, keepdims=True)
                result = (mixed / total).astype(BF16)
                for j in range(inner):
                    rows = result[j * tokens : (j + 1) * tokens]
                    if beside is None:
                        out_ref[r_out * inner + j] = rows
                    else:
                        out_ref[r_out * inner + j, 0] = refs[4][r_out * inner + j]
                        out_ref[r_out * inner + j, 1] = rows

        def whole(count):
            a, b = (scores_a, top_a), (scores_b, top_b)
            phase(a + (0,), None, count)

            def step(i, carry):
                phase(b + (2 * i + 1,), a + (2 * i,), count)
                phase(a + (2 * i + 2,), b + (2 * i + 1,), count)
                return carry

            lax.fori_loop(0, blocks // 2 - 1, step, 0)
            phase(b + (blocks - 1,), a + (blocks - 2,), count)
            phase(None, b + (blocks - 1,), count)

        @pl.when(scalar_ref[3] > 0)
        def _():
            whole(4 * per)

        @pl.when(scalar_ref[3] == 0)
        def _():
            whole(2 * per)

    operands = [queries, *pieces] + ([] if beside is None else [beside])
    out_dims = (CHIPS, tokens, HEAD_DIM) if beside is None else (CHIPS, 2, tokens, HEAD_DIM)
    return pl.pallas_call(
        kernel,
        in_specs=[SMEM] + [VMEM] * len(operands),
        out_specs=VMEM,
        out_shape=jax.ShapeDtypeStruct(out_dims, BF16),
        scratch_shapes=[
            pltpu.VMEM((rows_block, 4 * keys_each), F32),
            pltpu.VMEM((rows_block, 4 * keys_each), F32),
            pltpu.VMEM((rows_block, HEAD_DIM), F32),
            pltpu.VMEM((rows_block, HEAD_DIM), F32),
        ],
        cost_estimate=cost,
        compiler_params=pltpu.CompilerParams(vmem_limit_bytes=VMEM_LIMIT),
        name="attend",
    )(scalars, *operands)


def local(queries, keys, values, norm_gains):
    seq = lax.axis_size("seq")
    sections = lax.axis_size("section")
    here = lax.axis_index("seq")
    section = lax.axis_index("section")
    late = (section >= sections // 2).astype(jnp.int32)
    has_prior = (section > 0).astype(jnp.int32)
    scalars = jnp.stack([here // 8, here % 8 // 2, late, has_prior]).astype(jnp.int32)
    same_core = [[2 * p + c for p in range(CHIPS)] for c in range(2)]
    fence = lax.optimization_barrier

    def exchange(x):
        return lax.all_to_all(
            x, "seq", split_axis=0, concat_axis=0, tiled=True, axis_index_groups=same_core
        )

    def swap(x):
        return lax.ppermute(x, "seq", [(i, i ^ 1) for i in range(seq)])

    def passed_on(x, h):
        route = []
        for s in range(sections - 1):
            back = 8 * h if s + 1 == sections // 2 else 0
            for i in range(seq):
                route.append((s * seq + i, (s + 1) * seq + (i - back) % seq))
        return lax.ppermute(x, ("section", "seq"), route)

    sent_a, sent_b = prepare(scalars, queries[0], keys[0], values[0], norm_gains)
    first = exchange(sent_a)
    sent_b, first = fence((sent_b, first))
    own_a = first[:, :2]
    prior_a = passed_on(own_a, 0)
    own_b = exchange(sent_b)
    pieces_a = [first, swap(own_a), prior_a, swap(prior_a)]
    first, own_b, pieces_a[3] = fence((first, own_b, pieces_a[3]))
    prior_b = passed_on(own_b, 1)
    out_a = attend(scalars, first, 0, pieces_a)
    own_b_other = swap(own_b)
    prior_b, out_a = fence((prior_b, out_a))
    pieces_b = [own_b, own_b_other, prior_b, swap(prior_b)]
    back = exchange(attend(scalars, first, 1, pieces_b, out_a))
    return collect(scalars, back)[None]


def solution(mesh):
    return jax.shard_map(
        local,
        mesh=mesh,
        in_specs=(
            P("section", "seq", None),
            P("section", "seq", None),
            P("section", "seq", None),
            P(),
        ),
        out_specs=P("section", "seq", None),
        check_vma=False,
    )
```

time: 168 us -> 163 us (0.970)
  the two profiles are of different devices: /device:TPU:6 before, /device:TPU:32 now
where the time goes in v1:
time: 163 us; the launch traced here: 161 us
  blocking collectives  79.6 us (49%)
  Pallas kernels  37.7 us (23%)
  waiting for transfers between devices  32.7 us (20%)
  starting transfers between devices  9.81 us (6%)
    all_to_all x2, blocking collectives, exchange(): lax.all_to_all(x, 'seq', split_axis=0, concat_axis=0, tiled=True, axis_in...  79.6 us
    pallas_call x2, Pallas kernels, attend(): pl.pallas_call(kernel, in_specs=[SMEM] + [VMEM] * len(operands), out_spec...  31.7 us
    ppermute x2, waiting for transfers between devices, passed_on(): return lax.ppermute(x, ('section', 'seq'), route)  27.5 us
    ppermute x2, starting transfers between devices, passed_on(): return lax.ppermute(x, ('section', 'seq'), route)  5.3 us
    ppermute x4, waiting for transfers between devices, swap(): return lax.ppermute(x, 'seq', [(i, i ^ 1) for i in range(seq)])  5.27 us
    pallas_call x1, Pallas kernels, prepare(): pl.pallas_call(kernel, grid_spec=pltpu.PrefetchScalarGridSpec(num_scalar_...  4.39 us
    all_to_all x1, starting transfers between devices, exchange(): lax.all_to_all(x, 'seq', split_axis=0, concat_axis=0, tiled=True, axis_in...  3.78 us
  transfers between devices with their start and end apart: 7, of which 4 were waited for; matrix products, arithmetic and copies ran while one was open for 0% of the time, Pallas kernels for 10%

profile of v1, /device:TPU:32, one launch (start us, length us, event | category | flops | bytes accessed | tf_op | source)
XLA Modules:
  0.0 161.5 jit_solution(13450996588138195895)
XLA Ops:
  0.0 0.6 pad_add_fusion.scalar_ref
  0.6 4.4 %prepare.1 = (bf16[16,4,96,128]{3,2,1,0:T(8,128)(2,1)}, bf16[16,2,96,128]{3,2,1,0:T(8,128)(2,1)}) custom-call(s32[4]{0:T(128)} %pad_add_fusion.scalar_ref, bf16[96,4096]{1,0:T(8,128)(2,1)} %bitcast.8, bf16[96,4096]{1,0:T(8,128)(2,1)} %bitcast.9, bf16[96,4096]{1,0:T(8,128)(2,1)} %bitcast.10, f32[2,4096]{1,0:T(2,128)} %gain_ref.1), custom_call_target="tpu_custom_call" | custom-call | tf_op jit(solution)/shard_map/prepare/pallas_call | solution.py:53
  5.0 51.0 %all_to_all.15.query_ref.refs_0_ = bf16[16,4,96,128]{3,2,1,0:T(8,128)(2,1)S(1)} all-to-all(bf16[16,4,96,128]{3,2,1,0:T(8,128)(2,1)} %get-tuple-element.15), channel_id=1, replica_groups={{0,2,4,6,8,10,12,14,16,18,20,22,24,26,28,30},{1,3,5,7,9,11,13,15,17,19,..., dimensions={0} | all-to-all | bytes 3145728 | tf_op jit(solution)/shard_map/all_to_all | solution.py:211
  56.0 0.0 copy-start
  56.0 0.9 slice.3
  57.0 3.4 %collective-permute-start = (bf16[16,2,96,128]{3,2,1,0:T(8,128)(2,1)}, bf16[16,2,96,128]{3,2,1,0:T(8,128)(2,1)S(1)}, u32[]{:S(2)}, u32[]{:S(2)}) collective-permute-start(bf16[16,2,96,128]{3,2,1,0:T(8,128)(2,1)} %slice.3), channel_id=1, source_target_pairs={{0,32},{1,33},{2,34},{3,35},{4,36},{5,37},{6,38},{7,39},{8,40},{9,... | collective-permute-start | bytes 2359304 | tf_op jit(solution)/shard_map/ppermute | solution.py:224
  60.3 3.8 %all-to-all-start.1 = ((bf16[16,2,96,128]{3,2,1,0:T(8,128)(2,1)}), bf16[16,2,96,128]{3,2,1,0:T(8,128)(2,1)S(1)}, u32[]{:S(2)}, u32[]{:S(2)}) async-start(bf16[16,2,96,128]{3,2,1,0:T(8,128)(2,1)} %get-tuple-element.17), calls=%async_computation.1 | async-start | bytes 1572864 | tf_op jit(solution)/shard_map/all_to_all | solution.py:211
  64.1 22.2 %collective-permute-done.refs_2_ = bf16[16,2,96,128]{3,2,1,0:T(8,128)(2,1)S(1)} collective-permute-done((bf16[16,2,96,128]{3,2,1,0:T(8,128)(2,1)}, bf16[16,2,96,128]{3,2,1,0:T(8,128)(2,1)S(1)}, u32[]{:S(2)}, u32[]{:S(2)}) %collective-permute-start) | collective-permute-done | bytes 786464 | tf_op jit(solution)/shard_map/ppermute | solution.py:224
  86.4 0.0 collective-permute-start.1
  86.4 0.5 collective-permute-start.4
  86.9 0.0 all-to-all-done.1.refs_0_
  86.9 3.0 %collective-permute-done.1.refs_3_ = bf16[16,2,96,128]{3,2,1,0:T(8,128)(2,1)} collective-permute-done((bf16[16,2,96,128]{3,2,1,0:T(8,128)(2,1)S(1)}, bf16[16,2,96,128]{3,2,1,0:T(8,128)(2,1)}, u32[]{:S(2)}, u32[]{:S(2)}) %collective-permute-start.1) | collective-permute-done | bytes 786464 | tf_op jit(solution)/shard_map/ppermute | solution.py:216
  89.9 1.9 %collective-permute-start.3 = (bf16[16,2,96,128]{3,2,1,0:T(8,128)(2,1)S(1)}, bf16[16,2,96,128]{3,2,1,0:T(8,128)(2,1)S(1)}, u32[]{:S(2)}, u32[]{:S(2)}) collective-permute-start(bf16[16,2,96,128]{3,2,1,0:T(8,128)(2,1)S(1)} %all-to-all-done.1.refs_0_), channel_id=1, source_target_pairs={{0,32},{1,33},{2,34},{3,35},{4,36},{5,37},{6,38},{7,39},{8,40},{9,... | collective-permute-start | bytes 2359304 | tf_op jit(solution)/shard_map/ppermute | solution.py:224
  91.8 0.2 collective-permute-start.2
  92.0 0.0 collective-permute-done.4.refs_1_
  92.0 0.0 copy-done
  92.0 16.2 %attend.2.refs_4_ = bf16[16,96,128]{2,1,0:T(8,128)(2,1)S(1)} custom-call(s32[4]{0:T(128)S(1)} %copy-done, bf16[16,4,96,128]{3,2,1,0:T(8,128)(2,1)S(1)} %all_to_all.15.query_ref.refs_0_, bf16[16,4,96,128]{3,2,1,0:T(8,128)(2,1)S(1)} %all_to_all.15.query_ref.refs_0_, bf16[16,2,96,128]{3,2,1,0:T(8,128)(2,1)} %collective-permute-done.4.refs_1_, ...), custom_call_target="tpu_custom_call" | custom-call | flops 4831838208 | bytes 3145728 | tf_op jit(solution)/shard_map/attend/pallas_call | solution.py:182
  108.2 5.2 %collective-permute-done.3.refs_2_ = bf16[16,2,96,128]{3,2,1,0:T(8,128)(2,1)S(1)} collective-permute-done((bf16[16,2,96,128]{3,2,1,0:T(8,128)(2,1)S(1)}, bf16[16,2,96,128]{3,2,1,0:T(8,128)(2,1)S(1)}, u32[]{:S(2)}, u32[]{:S(2)}) %collective-permute-start.3) | collective-permute-done | bytes 786464 | tf_op jit(solution)/shard_map/ppermute | solution.py:224
  113.4 0.0 collective-permute-start.5
  113.4 0.0 collective-permute-done.2.refs_1_
  113.4 2.3 %collective-permute-done.5.refs_3_ = bf16[16,2,96,128]{3,2,1,0:T(8,128)(2,1)S(1)} collective-permute-done((bf16[16,2,96,128]{3,2,1,0:T(8,128)(2,1)S(1)}, bf16[16,2,96,128]{3,2,1,0:T(8,128)(2,1)S(1)}, u32[]{:S(2)}, u32[]{:S(2)}) %collective-permute-start.5) | collective-permute-done | bytes 786464 | tf_op jit(solution)/shard_map/ppermute | solution.py:216
  115.7 15.5 %attend.3 = bf16[16,2,96,128]{3,2,1,0:T(8,128)(2,1)S(1)} custom-call(s32[4]{0:T(128)S(1)} %copy-done, bf16[16,4,96,128]{3,2,1,0:T(8,128)(2,1)S(1)} %all_to_all.15.query_ref.refs_0_, bf16[16,2,96,128]{3,2,1,0:T(8,128)(2,1)S(1)} %all-to-all-done.1.refs_0_, bf16[16,2,96,128]{3,2,1,0:T(8,128)(2,1)S(1)} %collective-permute-done.2.refs_1_, ...), custom_call_target="tpu_custom_call" | custom-call | flops 4831838208 | bytes 3145728 | tf_op jit(solution)/shard_map/attend/pallas_call | solution.py:182
  131.2 28.6 %all_to_all.16.block_ref = bf16[16,2,96,128]{3,2,1,0:T(8,128)(2,1)S(1)} all-to-all(bf16[16,2,96,128]{3,2,1,0:T(8,128)(2,1)S(1)} %attend.3), channel_id=1, replica_groups={{0,2,4,6,8,10,12,14,16,18,20,22,24,26,28,30},{1,3,5,7,9,11,13,15,17,19,..., dimensions={0} | all-to-all | bytes 1572864 | tf_op jit(solution)/shard_map/all_to_all | solution.py:211
  159.9 1.6 collect.1
Async XLA Ops:
  56.0 36.0 %copy-start = (s32[4]{0:T(128)S(1)}, s32[4]{0:T(128)}, u32[]{:S(2)}) copy-start(s32[4]{0:T(128)} %pad_add_fusion.scalar_ref) | copy-start | bytes 52
  57.0 29.4 %collective-permute-start = (bf16[16,2,96,128]{3,2,1,0:T(8,128)(2,1)}, bf16[16,2,96,128]{3,2,1,0:T(8,128)(2,1)S(1)}, u32[]{:S(2)}, u32[]{:S(2)}) collective-permute-start(bf16[16,2,96,128]{3,2,1,0:T(8,128)(2,1)} %slice.3), channel_id=1, source_target_pairs={{0,32},{1,33},{2,34},{3,35},{4,36},{5,37},{6,38},{7,39},{8,40},{9,... | collective-permute-start | bytes 2359304 | tf_op jit(solution)/shard_map/ppermute | solution.py:224
  60.3 26.5 %all-to-all-start.1 = ((bf16[16,2,96,128]{3,2,1,0:T(8,128)(2,1)}), bf16[16,2,96,128]{3,2,1,0:T(8,128)(2,1)S(1)}, u32[]{:S(2)}, u32[]{:S(2)}) async-start(bf16[16,2,96,128]{3,2,1,0:T(8,128)(2,1)} %get-tuple-element.17), calls=%async_computation.1 | async-start | bytes 1572864 | tf_op jit(solution)/shard_map/all_to_all | solution.py:211
  86.4 3.5 %collective-permute-start.1 = (bf16[16,2,96,128]{3,2,1,0:T(8,128)(2,1)S(1)}, bf16[16,2,96,128]{3,2,1,0:T(8,128)(2,1)}, u32[]{:S(2)}, u32[]{:S(2)}) collective-permute-start(bf16[16,2,96,128]{3,2,1,0:T(8,128)(2,1)S(1)} %collective-permute-done.refs_2_), channel_id=1, source_target_pairs={{0,1},{1,0},{2,3},{3,2},{4,5},{5,4},{6,7},{7,6},{8,9},{9,8},{10,11... | collective-permute-start | bytes 2359304 | tf_op jit(solution)/shard_map/ppermute | solution.py:216
  86.4 5.6 %collective-permute-start.4 = (bf16[16,2,96,128]{3,2,1,0:T(8,128)(2,1)}, bf16[16,2,96,128]{3,2,1,0:T(8,128)(2,1)}, u32[]{:S(2)}, u32[]{:S(2)}) collective-permute-start(bf16[16,2,96,128]{3,2,1,0:T(8,128)(2,1)} %slice.3), channel_id=1, source_target_pairs={{0,1},{1,0},{2,3},{3,2},{4,5},{5,4},{6,7},{7,6},{8,9},{9,8},{10,11... | collective-permute-start | bytes 2359304 | tf_op jit(solution)/shard_map/ppermute | solution.py:216
  89.9 23.6 %collective-permute-start.3 = (bf16[16,2,96,128]{3,2,1,0:T(8,128)(2,1)S(1)}, bf16[16,2,96,128]{3,2,1,0:T(8,128)(2,1)S(1)}, u32[]{:S(2)}, u32[]{:S(2)}) collective-permute-start(bf16[16,2,96,128]{3,2,1,0:T(8,128)(2,1)S(1)} %all-to-all-done.1.refs_0_), channel_id=1, source_target_pairs={{0,32},{1,33},{2,34},{3,35},{4,36},{5,37},{6,38},{7,39},{8,40},{9,... | collective-permute-start | bytes 2359304 | tf_op jit(solution)/shard_map/ppermute | solution.py:224
  91.8 21.7 %collective-permute-start.2 = (bf16[16,2,96,128]{3,2,1,0:T(8,128)(2,1)S(1)}, bf16[16,2,96,128]{3,2,1,0:T(8,128)(2,1)S(1)}, u32[]{:S(2)}, u32[]{:S(2)}) collective-permute-start(bf16[16,2,96,128]{3,2,1,0:T(8,128)(2,1)S(1)} %all-to-all-done.1.refs_0_), channel_id=1, source_target_pairs={{0,1},{1,0},{2,3},{3,2},{4,5},{5,4},{6,7},{7,6},{8,9},{9,8},{10,11... | collective-permute-start | bytes 2359304 | tf_op jit(solution)/shard_map/ppermute | solution.py:216
  113.4 2.3 %collective-permute-start.5 = (bf16[16,2,96,128]{3,2,1,0:T(8,128)(2,1)S(1)}, bf16[16,2,96,128]{3,2,1,0:T(8,128)(2,1)S(1)}, u32[]{:S(2)}, u32[]{:S(2)}) collective-permute-start(bf16[16,2,96,128]{3,2,1,0:T(8,128)(2,1)S(1)} %collective-permute-done.3.refs_2_), channel_id=1, source_target_pairs={{0,1},{1,0},{2,3},{3,2},{4,5},{5,4},{6,7},{7,6},{8,9},{9,8},{10,11... | collective-permute-start | bytes 2359304 | tf_op jit(solution)/shard_map/ppermute | solution.py:216
